TPU v7x, 32 devices: a whole 2x2x4 slice. The times are simulated.
32 devices in a mesh: mu: 8 (over z, y), pa: 4 (over x, core).
Axes of the slice: x: 2, y: 2, z: 4, core: 2. Of those that a mesh axis runs over, the one named last changes fastest.
Arguments:
- three_center: bfloat16 [40, 64, 16384], P('mu', None, 'pa'), may hold values from -6 to 6
- pair_mu: int32 [8, 5], P('mu'), may hold values from 0 to 47
- pair_site: int32 [8, 5, 1], P('mu'), may hold values from 0 to 3; in each aligned block of 5 rows (0 to 4, 5 to 9, ..., all dimensions but the last counted through in order) at most 2 rows name the same one
- pair_pos: int32 [8, 5], P('mu'), may hold values from 0 to 11
- coeff: bfloat16 [3072, 2], replicated, may hold values from -0.21875 to 0.21875
- fitting: bfloat16 [48, 256, 256], P(None, 'pa'), as said below
Outputs:
- gfit: bfloat16 [8, 12, 1, 16384], P('mu', None, None, 'pa')
Inputs may be any that keep to these rules, and one draw needn't show every extreme that they name: `pair_site`: of the 5 pairs listed for one index of mu, at most 2 name the same site, and 2 is reached. Every fitting[b] is a symmetric matrix.
All inputs are finite; a program needn't handle non-finite values.
Results may differ from a plain program's by a relative error of at most 0.0058.
Values may be sent and summed in bfloat16 or wider, within the bound.
A program may use at most 64 MiB of HBM per device.

v0:
```python
import jax
import jax.numpy as jnp
from jax import lax
from jax.sharding import PartitionSpec as P

SITES = 4
NU_SITE = 12
CAP = 2


def local(three_center, pair_mu, pair_site, pair_pos, coeff, fitting):
    mu_size = lax.axis_size("mu")
    block_size = three_center.shape[1]
    slice_width = fitting.shape[1]
    pair_count = three_center.shape[0]
    groups = mu_size // SITES
    orbitals = coeff.shape[1]
    per_group = orbitals // groups
    mu_blocks = coeff.shape[0] // block_size
    mu_rows = coeff.reshape(mu_blocks, block_size, orbitals)[pair_mu[0]]
    pieces = jnp.einsum(
        "tmo,tmx->tox", mu_rows, three_center, preferred_element_type=jnp.float32
    ).astype(jnp.bfloat16)
    columns = pieces.shape[2]
    site_ids = pair_site[0, :, 0]
    positions = pair_pos[0]
    indices = jnp.arange(pair_count, dtype=jnp.int32)
    earlier = (site_ids[:, None] == site_ids[None, :]) & (indices[:, None] > indices[None, :])
    slot_rank = jnp.sum(earlier.astype(jnp.int32), axis=1)
    slot_ids = site_ids * CAP + slot_rank
    selected = slot_ids[:, None] == jnp.arange(SITES * CAP, dtype=jnp.int32)[None, :]
    slot_keys = jnp.sum(jnp.where(selected, positions[:, None] + 1, 0), axis=0) - 1
    outgoing = jnp.einsum(
        "tk,tgx->gkx", selected.astype(jnp.bfloat16), pieces, preferred_element_type=jnp.float32
    ).astype(jnp.bfloat16)
    outgoing = outgoing.reshape(mu_size, CAP, per_group, columns)
    key_rows = jnp.tile(slot_keys.reshape(SITES, CAP), (groups, 1))
    key_grid = key_rows[:, :, None]
    arrived = lax.all_to_all(outgoing, "mu", split_axis=0, concat_axis=0, tiled=True)
    arrived_keys = lax.all_to_all(key_grid, "mu", split_axis=0, concat_axis=0, tiled=True)
    item_count = arrived.shape[2]
    flat_keys = arrived_keys[:, :, 0].reshape(-1)
    onehot = (flat_keys[None, :] == jnp.arange(NU_SITE, dtype=jnp.int32)[:, None]).astype(
        jnp.bfloat16
    )
    summed = jnp.dot(
        onehot, arrived.reshape(-1, item_count * columns), preferred_element_type=jnp.float32
    )
    fitted = summed.reshape(NU_SITE, item_count, columns).astype(jnp.bfloat16)
    my_site = lax.axis_index("mu") % SITES
    weights = lax.dynamic_index_in_dim(
        fitting.reshape(SITES, NU_SITE, slice_width, fitting.shape[2]), my_site, 0, keepdims=False
    )
    local_rows = fitted.reshape(NU_SITE, per_group, block_size, slice_width)
    partial_sum = jnp.einsum(
        "kina,kaq->kinq", local_rows, weights, preferred_element_type=jnp.float32
    )
    summed_all = lax.psum(partial_sum, "pa")
    owned_cols = lax.dynamic_slice_in_dim(
        summed_all, lax.axis_index("pa") * slice_width, slice_width, 3
    )
    result = owned_cols.reshape(NU_SITE, per_group, block_size * slice_width)
    return result.astype(jnp.bfloat16)[None]


def solution(mesh):
    in_specs = (
        P("mu", None, "pa"),
        P("mu", None),
        P("mu", None, None),
        P("mu", None),
        P(),
        P(None, "pa", None),
    )
    out_specs = P("mu", None, None, "pa")
    return jax.shard_map(local, mesh=mesh, in_specs=in_specs, out_specs=out_specs, check_vma=False)
```

profile of v0, /device:TPU:0, one launch (start us, length us, event | category | flops | bytes accessed | tf_op | source)
XLA Modules:
  0.0 51.6 jit_solution(7242579657425354149)
XLA Ops:
  0.0 0.0 copy-start
  0.0 0.8 %add_bitcast_fusion = s32[5]{0:T(128)S(1)} fusion(s32[1,5]{1,0:T(1,128)} %param.9), kind=kLoop, calls=%fused_computation.22 | loop fusion | flops 5 | bytes 40 | tf_op jit(solution)/shard_map/add | solution.py:32
  0.8 0.9 %convert_reduce_fusion = s32[5]{0:T(128)S(1)} fusion(s32[5]{0:T(128)} %bitcast.35), kind=kLoop, calls=%fused_computation.16 | loop fusion | flops 120 | bytes 40 | tf_op jit(solution)/shard_map/reduce_sum | solution.py:29
  1.7 0.7 %multiply_add_fusion = s32[5]{0:T(128)S(1)} fusion(s32[5]{0:T(128)S(1)} %convert_reduce_fusion, s32[1,5,1]{1,2,0:T(1,128)} %param.8), kind=kLoop, calls=%fused_computation.24 | loop fusion | flops 10 | bytes 60 | tf_op jit(solution)/shard_map/add | solution.py:30
  2.4 0.1 select_reduce_fusion
  2.5 0.1 sub.6
  2.6 0.6 %tile.7.clone = s32[2,4,2]{2,1,0:T(4,128)} broadcast(s32[4,2]{1,0:T(4,128)S(1)} %sub.6), dimensions={1,2} | broadcast | bytes 96 | tf_op jit(solution)/shard_map/tile | solution.py:37
  3.2 7.3 %all-to-all-start = ((s32[8,2,1]{1,2,0:T(1,128)}), s32[8,2,1]{1,2,0:T(1,128)S(1)}, u32[]{:S(2)}, u32[]{:S(2)}) async-start(s32[8,2,1]{1,2,0:T(1,128)} %bitcast.2), calls=%async_computation | async-start | bytes 8192 | tf_op jit(solution)/shard_map/all_to_all | solution.py:40
  10.5 0.7 %fusion.9 = s32[5]{0:T(128)S(1)} fusion(s32[1,5]{1,0:T(1,128)} %param.7), kind=kLoop, calls=%fused_computation.21 | loop fusion | flops 15 | bytes 40 | tf_op jit(solution)/shard_map/select_n | solution.py:20
  11.1 0.8 %reshape.96 = bf16[48,64,2]{1,0,2:T(8,128)(2,1)S(1)} reshape(bf16[3072,2]{0,1:T(2,128)(2,1)} %param.10) | data formatting | bytes 24576 | tf_op jit(solution)/shard_map/reshape | solution.py:20
  12.0 0.6 %gather_fusion = bf16[5,64,2]{1,2,0:T(2,128)(2,1)S(1)} fusion(bf16[48,64,2]{1,2,0:T(2,128)(2,1)S(1)} %copy.22, s32[1024]{0:T(1024)S(1)} %pad_clamp_fusion), kind=kCustom, calls=%fused_computation | custom fusion | bytes 2580 | tf_op jit(solution)/shard_map/gather | solution.py:20
  12.5 0.0 copy-done
  12.5 0.5 convolution_convert_fusion.2
  13.0 0.2 fusion
  13.2 0.8 %reshape.97 = bf16[8,2,1,4096]{3,1,0,2:T(2,128)(2,1)} reshape(bf16[2,8,4096]{2,1,0:T(8,128)(2,1)S(1)} %fusion) | data formatting | bytes 262144 | tf_op jit(solution)/shard_map/reshape | solution.py:36
  13.9 3.0 %all-to-all-done = s32[8,2,1]{1,2,0:T(1,128)S(1)} async-done(((s32[8,2,1]{1,2,0:T(1,128)}), s32[8,2,1]{1,2,0:T(1,128)S(1)}, u32[]{:S(2)}, u32[]{:S(2)}) %all-to-all-start) | async-done | bytes 96 | tf_op jit(solution)/shard_map/all_to_all | solution.py:40
  16.9 3.4 %all-to-all-start.1 = ((bf16[8,2,1,4096]{3,1,2,0:T(2,128)(2,1)}), bf16[8,2,1,4096]{3,1,2,0:T(2,128)(2,1)S(1)}, u32[]{:S(2)}, u32[]{:S(2)}) async-start(bf16[8,2,1,4096]{3,1,2,0:T(2,128)(2,1)} %bitcast.7), calls=%async_computation.1 | async-start | bytes 262144 | tf_op jit(solution)/shard_map/all_to_all | solution.py:39
  20.3 0.6 %broadcast.68 = s32[]{:T(128)} broadcast(s32[]{:T(128)} %constant.16.clone.1), dimensions={} | broadcast | bytes 8 | tf_op jit(solution)/shard_map/all_to_all | solution.py:40
  20.9 0.7 %reduce.3 = s32[8,2]{1,0:T(8,128)S(1)} reduce(s32[8,2,1]{1,2,0:T(1,128)S(1)} %all-to-all-done, s32[]{:T(128)} %broadcast.68), dimensions={2}, to_apply=%all_to_all.6.reduce_sub_computation.3 | reduce | bytes 132 | tf_op jit(solution)/shard_map/all_to_all | solution.py:40
  21.6 0.1 eq.49
  21.7 5.9 %all-to-all-done.1 = bf16[8,2,1,4096]{3,1,2,0:T(2,128)(2,1)S(1)} async-done(((bf16[8,2,1,4096]{3,1,2,0:T(2,128)(2,1)}), bf16[8,2,1,4096]{3,1,2,0:T(2,128)(2,1)S(1)}, u32[]{:S(2)}, u32[]{:S(2)}) %all-to-all-start.1) | async-done | bytes 131104 | tf_op jit(solution)/shard_map/all_to_all | solution.py:39
  27.6 0.1 reshape.98
  27.7 0.2 convolution_convert_fusion
  27.8 0.9 %reshape.99 = bf16[12,64,64]{2,1,0:T(8,128)(2,1)} reshape(bf16[12,4096]{1,0:T(8,128)(2,1)S(1)} %convolution_convert_fusion) | data formatting | bytes 196608 | tf_op jit(solution)/shard_map/reshape.1
  28.7 1.3 %convolution_bitcast_fusion = f32[12,1,64,256]{3,2,0,1:T(8,128)S(1)} fusion(bf16[12,64,64]{2,1,0:T(8,128)(2,1)} %reshape.99, bf16[4,12,64,256]{3,2,1,0:T(8,128)(2,1)} %bitcast.34, s32[]{:T(128)S(6)} %select_n.31), kind=kOutput, calls=%fused_computation.5 | convolution fusion | flops 25165824 | bytes 1376260 | tf_op jit(solution)/shard_map/kina,kaq->kinq/dot_general | solution.py:55
  30.0 19.7 %all-reduce.1 = bf16[12,1,64,256]{3,2,0,1:T(8,128)(2,1)} all-reduce(f32[12,1,64,256]{3,2,0,1:T(8,128)S(1)} %convolution_bitcast_fusion), channel_id=1, replica_groups=mesh['mu'=8,'pa'=4] {'pa'}, use_global_device_ids=true, to_apply=%region_2.3 | all-reduce | flops 196608 | bytes 1179648 | tf_op jit(solution)/shard_map/psum | solution.py:58
  49.7 1.0 %dynamic-slice_convert_fusion = bf16[12,1,64,64]{3,2,0,1:T(8,128)(2,1)S(1)} fusion(bf16[12,1,64,256]{3,2,0,1:T(8,128)(2,1)} %all-reduce.1, s32[]{:T(128)S(6)} %select_n.32), kind=kLoop, calls=%fused_computation.7 | loop fusion | bytes 196612 | tf_op jit(solution)/shard_map/convert_element_type | solution.py:63
  50.8 0.8 %convert_element_type.39 = bf16[1,12,1,4096]{3,1,2,0:T(8,128)(2,1)} reshape(bf16[12,1,64,64]{3,2,0,1:T(8,128)(2,1)S(1)} %dynamic-slice_convert_fusion) | data formatting | bytes 196608 | tf_op jit(solution)/shard_map/convert_element_type | solution.py:63
  (3 shorter events, 0.0 us)
Async XLA Ops:
  0.0 12.5 %copy-start = (bf16[5,64,4096]{2,1,0:T(8,128)(2,1)S(1)}, bf16[5,64,4096]{2,1,0:T(8,128)(2,1)}, u32[]{:S(2)}) copy-start(bf16[5,64,4096]{2,1,0:T(8,128)(2,1)} %param.6) | copy-start | bytes 7864324
  3.2 13.7 %all-to-all-start = ((s32[8,2,1]{1,2,0:T(1,128)}), s32[8,2,1]{1,2,0:T(1,128)S(1)}, u32[]{:S(2)}, u32[]{:S(2)}) async-start(s32[8,2,1]{1,2,0:T(1,128)} %bitcast.2), calls=%async_computation | async-start | bytes 8192 | tf_op jit(solution)/shard_map/all_to_all | solution.py:40
  16.9 10.7 %all-to-all-start.1 = ((bf16[8,2,1,4096]{3,1,2,0:T(2,128)(2,1)}), bf16[8,2,1,4096]{3,1,2,0:T(2,128)(2,1)S(1)}, u32[]{:S(2)}, u32[]{:S(2)}) async-start(bf16[8,2,1,4096]{3,1,2,0:T(2,128)(2,1)} %bitcast.7), calls=%async_computation.1 | async-start | bytes 262144 | tf_op jit(solution)/shard_map/all_to_all | solution.py:39
where the time goes:
time: 52.1 us; the launch traced here: 51.6 us
  blocking collectives  19.7 us (38%)
  starting transfers between devices  10.7 us (21%)
  waiting for transfers between devices  8.88 us (17%)
  local copies, waits for them, and re-layouts  6.33 us (12%)
  other arithmetic  3.87 us (7%)
  matrix products  2.12 us (4%)
    psum x1, blocking collectives, local(): summed_all = lax.psum(partial_sum, 'pa')  19.7 us
    all_to_all x1, starting transfers between devices, local(): lax.all_to_all(key_grid, 'mu', split_axis=0, concat_axis=0, tiled=True)  7.28 us
    all_to_all x1, waiting for transfers between devices, local(): lax.all_to_all(outgoing, 'mu', split_axis=0, concat_axis=0, tiled=True)  5.88 us
    all_to_all x1, starting transfers between devices, local(): lax.all_to_all(outgoing, 'mu', split_axis=0, concat_axis=0, tiled=True)  3.37 us
    all_to_all x1, waiting for transfers between devices, local(): lax.all_to_all(key_grid, 'mu', split_axis=0, concat_axis=0, tiled=True)  3 us
    convert_element_type x2, local copies, waits for them, and re-layouts, local(): return result.astype(jnp.bfloat16)[None]  1.89 us
    dot_general x1, matrix products, local(): jnp.einsum('kina,kaq->kinq', local_rows, weights, preferred_element_type=...  1.33 us
  transfers between devices with their start and end apart: 2, of which 2 were waited for; matrix products, arithmetic and copies ran while one was open for 9% of the time, Pallas kernels for 0%

commit v1 on v0

v1 whole, which is shorter than its diff:
```python
import functools

import jax
import jax.numpy as jnp
from jax import lax
from jax.experimental import pallas as pl
from jax.experimental.pallas import tpu as pltpu
from jax.sharding import PartitionSpec as P

SITES = 4
NU_SITE = 12
CAP = 2
SLOTS = SITES * CAP
LANES = 128
CHUNKS = 2
MESH = pl.DeviceIdType.MESH
F32 = jnp.float32
BF16 = jnp.bfloat16


def loop(count, body, carry):
    if count <= 16:
        for step in range(count):
            carry = body(step, carry)
        return carry
    return lax.fori_loop(0, count, body, carry)


def kernel(
    n, mu_ref, site_ref, pos_ref, coeff_ref, tc_hbm, fit_hbm, out_ref,
    tc, fit, turned, payload, arrived, keys_out, keys_in, gath, weights, total,
    tc_sem, fit_sem, key_send, key_recv, pay_send, pay_recv,
    x_send, x_recv, sib_send, sib_recv, fwd_send, fwd_recv,
):
    me = lax.axis_index("mu")
    shard = lax.axis_index("pa")
    sibling = shard + 1 - 2 * lax.rem(shard, 2)
    across = lax.rem(shard + 2, 4)
    diagonal = lax.rem(sibling + 2, 4)
    pairs, block, _ = tc.shape
    width = tc.shape[2] // CHUNKS
    rows = width // LANES
    groups = coeff_ref.shape[1]

    def tc_copy(c):
        columns = pl.ds(c * width, width)
        return pltpu.make_async_copy(
            tc_hbm.at[:, :, columns], tc.at[:, :, columns], tc_sem.at[c]
        )

    for c in range(CHUNKS):
        tc_copy(c).start()
    site = lax.rem(me, SITES)
    fit_copy = pltpu.make_async_copy(
        fit_hbm.at[pl.ds(site * NU_SITE, NU_SITE)], fit, fit_sem
    )
    fit_copy.start()

    barrier = pltpu.get_barrier_semaphore()

    def greet(d, carry):
        pl.semaphore_signal(
            barrier, inc=1, device_id={"mu": lax.rem(me + d + 1, n)}, device_id_type=MESH
        )
        return carry

    loop(n - 1, greet, 0)
    for peer in (sibling, across, diagonal):
        pl.semaphore_signal(barrier, inc=1, device_id={"pa": peer}, device_id_type=MESH)

    slots = []
    for t in range(pairs):
        rank = jnp.int32(0)
        for u in range(t):
            rank += (site_ref[0, u] == site_ref[0, t]).astype(jnp.int32)
        slots.append(site_ref[0, t] * CAP + rank)
    key_row = lax.broadcasted_iota(jnp.int32, (SLOTS, LANES), 0)
    table = jnp.full((SLOTS, LANES), -1.0, F32)
    for t in range(pairs):
        table = jnp.where(key_row == slots[t], pos_ref[0, t].astype(F32), table)
    keys_out[...] = table
    keys_in[0] = table
    slot_row = lax.broadcasted_iota(jnp.int32, (groups, SLOTS, LANES), 1).reshape(
        groups * SLOTS, LANES
    )
    lane = lax.broadcasted_iota(jnp.int32, (groups * SLOTS, LANES), 1)
    halves = []
    for t in range(pairs):
        mu = mu_ref[0, t]
        two = coeff_ref[lax.shift_right_logical(mu, 1)].astype(F32)
        wide = jnp.broadcast_to(two[:, None, :], (groups, SLOTS, LANES))
        wide = wide.reshape(groups * SLOTS, LANES)
        moved = lax.bitwise_and(mu + t, 1) == 1
        wide = jnp.where(moved, pltpu.roll(wide, block, 1), wide)
        halves.append(jnp.where(slot_row == slots[t], wide, 0.0))
    left = []
    for t in range(0, pairs, 2):
        if t + 1 < pairs:
            left.append(jnp.where(lane < block, halves[t], halves[t + 1]).astype(BF16))
        else:
            left.append(halves[t][:, :block].astype(BF16))

    def key_copy(d):
        return pltpu.make_async_remote_copy(
            src_ref=keys_out, dst_ref=keys_in.at[d],
            send_sem=key_send.at[d], recv_sem=key_recv.at[d],
            device_id={"mu": lax.rem(me + d, n)}, device_id_type=MESH,
        )

    def pay_copy(c, d):
        owner = lax.rem(me + d, n)
        return pltpu.make_async_remote_copy(
            src_ref=payload.at[c, owner], dst_ref=arrived.at[c, d],
            send_sem=pay_send.at[c, d], recv_sem=pay_recv.at[c, d],
            device_id={"mu": owner}, device_id_type=MESH,
        )

    def make_payload(c):
        tc_copy(c).wait()
        for j in range(0, rows, 2):
            start = c * width + j * LANES
            acc = None
            for t, part in zip(range(0, pairs, 2), left):
                depth = part.shape[1]
                right = tc[t:t + depth // block, :, start:start + 2 * LANES]
                term = jnp.dot(
                    part, right.reshape(depth, 2 * LANES), preferred_element_type=F32
                )
                acc = term if acc is None else acc + term
            turned[pl.ds(j, n * CAP, stride=rows), :] = acc[:, :LANES]
            turned[pl.ds(j + 1, n * CAP, stride=rows), :] = acc[:, LANES:]

        def pack(w, carry):
            first = w * CAP * rows
            if not isinstance(w, int):
                first = pl.multiple_of(first, CAP * rows)
            payload[c, w] = turned[pl.ds(first, CAP * rows), :].astype(BF16)
            return carry

        loop(n, pack, 0)
        arrived[c, 0] = payload[c, me]

    order = list(range(1, n))
    if n <= 16:
        order.sort(key=lambda d: abs(d - n // 2))

    def each_peer(act):
        if n <= 16:
            for d in order:
                act(d)
        else:
            def body(d, carry):
                act(d)
                return carry
            lax.fori_loop(1, n, body, 0)

    for c in range(CHUNKS):
        make_payload(c)
        if c == 0:
            pl.semaphore_wait(barrier, n - 1 + 3)
            each_peer(lambda d: key_copy(d).start())
        each_peer(lambda d, c=c: pay_copy(c, d).start())

    fit_copy.wait()
    for k in range(NU_SITE):
        double = jnp.concatenate([fit[k], fit[k]], axis=0)
        flipped = double.T
        lane_w = lax.broadcasted_iota(jnp.int32, (block, 2 * block), 1)
        for q in range(4):
            piece = flipped[q * block:(q + 1) * block, :]
            zero = jnp.zeros_like(piece)
            weights[k, q, 0:block, :] = jnp.where(lane_w < block, piece, zero)
            weights[k, q, block:2 * block, :] = jnp.where(lane_w < block, zero, piece)

    each_peer(lambda d: key_copy(d).wait_recv())

    def pa_copy(c, which, target, send, recv):
        return pltpu.make_async_remote_copy(
            src_ref=gath.at[c, which], dst_ref=gath.at[c, which],
            send_sem=send.at[c], recv_sem=recv.at[c],
            device_id={"pa": target}, device_id_type=MESH,
        )

    def x_copy(c):
        return pa_copy(c, shard, across, x_send, x_recv)

    def sib_copy(c):
        return pa_copy(c, shard, sibling, sib_send, sib_recv)

    def fwd_copy(c):
        return pa_copy(c, across, sibling, fwd_send, fwd_recv)

    for c in range(CHUNKS):
        def add_source(d, sums, c=c):
            if n > 16 or d:
                pass
            sums = list(sums)
            for cap in range(CAP):
                key = keys_in[d, pl.ds(site * CAP + cap, 1), :]
                value = arrived[c, d, cap * rows:(cap + 1) * rows, :].astype(F32)
                for k in range(NU_SITE):
                    sums[k] = sums[k] + jnp.where(key == float(k), value, 0.0)
            return tuple(sums)

        sums = tuple(jnp.zeros((rows, LANES), F32) for _ in range(NU_SITE))
        if n <= 16:
            sums = add_source(0, sums)
            for d in reversed(order):
                pay_copy(c, d).wait_recv()
                sums = add_source(d, sums)
        else:
            each_peer(lambda d, c=c: pay_copy(c, d).wait_recv())
            sums = lax.fori_loop(0, n, add_source, sums)
        for k in range(NU_SITE):
            gath[c, shard, k] = sums[k].astype(BF16)
        x_copy(c).start()
        sib_copy(c).start()

    def product(k, chip):
        lines = [
            jnp.concatenate([gath[c, 2 * chip, k], gath[c, 2 * chip + 1, k]], axis=1)
            for c in range(CHUNKS)
        ]
        held = weights[k, pl.ds(2 * chip, 2)].reshape(4 * block, LANES)
        return jnp.dot(jnp.concatenate(lines, axis=0), held, preferred_element_type=F32)

    chip = lax.div(shard, 2)
    for c in range(CHUNKS):
        x_copy(c).wait_recv()
        fwd_copy(c).start()
        sib_copy(c).wait_recv()
    for k in range(NU_SITE):
        total[k] = product(k, chip)
    for c in range(CHUNKS):
        fwd_copy(c).wait_recv()
    for k in range(NU_SITE):
        out_ref[k] = (total[k] + product(k, 1 - chip)).astype(BF16)

    each_peer(lambda d: key_copy(d).wait_send())
    for c in range(CHUNKS):
        each_peer(lambda d, c=c: pay_copy(c, d).wait_send())
        x_copy(c).wait_send()
        sib_copy(c).wait_send()
        fwd_copy(c).wait_send()


def local(three_center, pair_mu, pair_site, pair_pos, coeff, fitting):
    n = lax.axis_size("mu")
    pairs, block, columns = three_center.shape
    orbitals = coeff.shape[1]
    shards = lax.axis_size("pa")
    rows = columns // CHUNKS // LANES
    pair_blocks = coeff.reshape(coeff.shape[0] // LANES, LANES, orbitals).transpose(0, 2, 1)
    smem = pl.BlockSpec(memory_space=pltpu.SMEM)
    vmem = pl.BlockSpec(memory_space=pltpu.VMEM)
    hbm = pl.BlockSpec(memory_space=pltpu.HBM)
    dma = pltpu.SemaphoreType.DMA
    result = pl.pallas_call(
        functools.partial(kernel, n),
        out_shape=jax.ShapeDtypeStruct((NU_SITE, columns // LANES, LANES), BF16),
        in_specs=[smem, smem, smem, vmem, hbm, hbm],
        out_specs=vmem,
        scratch_shapes=[
            pltpu.VMEM((pairs, block, columns), BF16),
            pltpu.VMEM((NU_SITE,) + fitting.shape[1:], BF16),
            pltpu.VMEM((n * CAP * rows, LANES), F32),
            pltpu.VMEM((CHUNKS, n, CAP * rows, LANES), BF16),
            pltpu.VMEM((CHUNKS, n, CAP * rows, LANES), BF16),
            pltpu.VMEM((SLOTS, LANES), F32),
            pltpu.VMEM((n, SLOTS, LANES), F32),
            pltpu.VMEM((CHUNKS, shards, NU_SITE, rows, LANES), BF16),
            pltpu.VMEM((NU_SITE, shards, 2 * block, LANES), BF16),
            pltpu.VMEM((NU_SITE, columns // LANES, LANES), F32),
            dma((CHUNKS,)), dma,
            dma((n,)), dma((n,)), dma((CHUNKS, n)), dma((CHUNKS, n)),
            dma((CHUNKS,)), dma((CHUNKS,)), dma((CHUNKS,)),
            dma((CHUNKS,)), dma((CHUNKS,)), dma((CHUNKS,)),
        ],
        compiler_params=pltpu.CompilerParams(
            collective_id=0, has_side_effects=True, vmem_limit_bytes=40 * 1024 * 1024
        ),
    )(pair_mu, pair_site[:, :, 0], pair_pos, pair_blocks, three_center, fitting)
    shape = (NU_SITE, CHUNKS * rows * LANES)
    return result.reshape((1, NU_SITE, 1, shape[1]))


def solution(mesh):
    in_specs = (
        P("mu", None, "pa"),
        P("mu", None),
        P("mu", None, None),
        P("mu", None),
        P(),
        P(None, "pa", None),
    )
    out_specs = P("mu", None, None, "pa")
    return jax.shard_map(local, mesh=mesh, in_specs=in_specs, out_specs=out_specs, check_vma=False)
```

time: 52.1 us -> 23.3 us (0.45)
  the two profiles are of different devices: /device:TPU:0 before, /device:TPU:1 now
where the time goes in v1:
time: 23.3 us; the launch traced here: 23.1 us
  Pallas kernels  16.5 us (71%)
  local copies, waits for them, and re-layouts  6.55 us (28%)
    pallas_call x1, Pallas kernels, local(): pl.pallas_call(functools.partial(kernel, n), out_shape=jax.ShapeDtypeStru...  16.5 us
    unnamed x12, local copies, waits for them, and re-layouts  5.82 us
    reshape x1, local copies, waits for them, and re-layouts, local(): return result.reshape((1, NU_SITE, 1, shape[1]))  0.74 us

profile of v1, /device:TPU:1, one launch (start us, length us, event | category | flops | bytes accessed | tf_op | source)
XLA Modules:
  0.0 23.1 jit_solution(9793649990648936695)
XLA Ops:
  0.0 0.0 copy-start
  0.0 1.7 %copy-done = bf16[5,64,4096]{2,1,0:T(8,128)(2,1)S(1)} copy-done((bf16[5,64,4096]{2,1,0:T(8,128)(2,1)S(1)}, bf16[5,64,4096]{2,1,0:T(8,128)(2,1)}, u32[]{:S(2)}) %copy-start) | copy-done | bytes 2621464
  1.7 0.0 copy-start.1
  1.7 1.4 %copy-done.1 = bf16[48,64,256]{2,1,0:T(8,128)(2,1)S(1)} copy-done((bf16[48,64,256]{2,1,0:T(8,128)(2,1)S(1)}, bf16[48,64,256]{2,1,0:T(8,128)(2,1)}, u32[]{:S(2)}) %copy-start.1) | copy-done | bytes 1572888
  3.1 0.0 copy-start.2
  3.2 0.7 %copy-done.2 = bf16[3072,2]{0,1:T(2,128)(2,1)S(1)} copy-done((bf16[3072,2]{0,1:T(2,128)(2,1)S(1)}, bf16[3072,2]{0,1:T(2,128)(2,1)}, u32[]{:S(2)}) %copy-start.2) | copy-done | bytes 12312
  3.9 0.0 copy-start.3
  3.9 0.7 %copy-done.3 = s32[1,5]{1,0:T(1,128)S(1)} copy-done((s32[1,5]{1,0:T(1,128)S(1)}, s32[1,5]{1,0:T(1,128)}, u32[]{:S(2)}) %copy-start.3) | copy-done | bytes 44
  4.5 0.0 copy-start.4
  4.5 0.7 %copy-done.4 = s32[1,5,1]{1,2,0:T(1,128)S(1)} copy-done((s32[1,5,1]{1,2,0:T(1,128)S(1)}, s32[1,5,1]{1,2,0:T(1,128)}, u32[]{:S(2)}) %copy-start.4) | copy-done | bytes 44
  5.2 0.0 copy-start.5
  5.2 0.7 %copy-done.5 = s32[1,5]{1,0:T(1,128)S(1)} copy-done((s32[1,5]{1,0:T(1,128)S(1)}, s32[1,5]{1,0:T(1,128)}, u32[]{:S(2)}) %copy-start.5) | copy-done | bytes 44
  5.8 16.5 %shard_map.64 = bf16[12,32,128]{2,1,0:T(8,128)(2,1)S(1)} custom-call(s32[1,5]{1,0:T(1,128)S(1)} %copy-done.3, s32[1,5]{1,0:T(1,128)S(1)} %bitcast.5, s32[1,5]{1,0:T(1,128)S(1)} %copy-done.5, bf16[24,2,128]{2,1,0:T(2,128)(2,1)S(1)} %bitcast.4, bf16[5,64,4096]{2,1,0:T(8,128)(2,1)S(1)} %copy-done, bf16[48,64,256]{2,1,0:T(8,128)(2,1)S(1)} %copy-done.1), custom_call_target="tpu_custom_call" | custom-call | tf_op jit(solution)/shard_map/pallas_call | solution.py:258
  22.3 0.7 %reshape.7 = bf16[1,12,1,4096]{3,1,2,0:T(8,128)(2,1)} reshape(bf16[12,32,128]{2,1,0:T(8,128)(2,1)S(1)} %shard_map.64) | data formatting | bytes 196608 | tf_op jit(solution)/shard_map/reshape | solution.py:284
Async XLA Ops:
  0.0 1.7 %copy-start = (bf16[5,64,4096]{2,1,0:T(8,128)(2,1)S(1)}, bf16[5,64,4096]{2,1,0:T(8,128)(2,1)}, u32[]{:S(2)}) copy-start(bf16[5,64,4096]{2,1,0:T(8,128)(2,1)} %tc_hbm.1) | copy-start | bytes 7864324
  1.7 1.4 %copy-start.1 = (bf16[48,64,256]{2,1,0:T(8,128)(2,1)S(1)}, bf16[48,64,256]{2,1,0:T(8,128)(2,1)}, u32[]{:S(2)}) copy-start(bf16[48,64,256]{2,1,0:T(8,128)(2,1)} %fit_hbm.1) | copy-start | bytes 4718596
  3.1 0.7 %copy-start.2 = (bf16[3072,2]{0,1:T(2,128)(2,1)S(1)}, bf16[3072,2]{0,1:T(2,128)(2,1)}, u32[]{:S(2)}) copy-start(bf16[3072,2]{0,1:T(2,128)(2,1)} %param.10) | copy-start | bytes 36868
  3.9 0.7 %copy-start.3 = (s32[1,5]{1,0:T(1,128)S(1)}, s32[1,5]{1,0:T(1,128)}, u32[]{:S(2)}) copy-start(s32[1,5]{1,0:T(1,128)} %mu_ref.1) | copy-start | bytes 64
  4.5 0.7 %copy-start.4 = (s32[1,5,1]{1,2,0:T(1,128)S(1)}, s32[1,5,1]{1,2,0:T(1,128)}, u32[]{:S(2)}) copy-start(s32[1,5,1]{1,2,0:T(1,128)} %param.8) | copy-start | bytes 64
  5.2 0.7 %copy-start.5 = (s32[1,5]{1,0:T(1,128)S(1)}, s32[1,5]{1,0:T(1,128)}, u32[]{:S(2)}) copy-start(s32[1,5]{1,0:T(1,128)} %pos_ref.1) | copy-start | bytes 64

commit v2 on v1

--- a/solution.py
+++ b/solution.py
@@ -13,6 +13,7 @@
 SLOTS = SITES * CAP
 LANES = 128
 CHUNKS = 2
+VMEM_BYTES = 60 * 1000000
 MESH = pl.DeviceIdType.MESH
 F32 = jnp.float32
 BF16 = jnp.bfloat16
@@ -27,9 +28,9 @@
 
 
 def kernel(
-    n, mu_ref, site_ref, pos_ref, coeff_ref, tc_hbm, fit_hbm, out_ref,
-    tc, fit, turned, payload, arrived, keys_out, keys_in, gath, weights, total,
-    tc_sem, fit_sem, key_send, key_recv, pay_send, pay_recv,
+    n, mu_hbm, site_hbm, pos_hbm, coeff_hbm, tc_hbm, fit_hbm, out_ref,
+    mu_ref, site_ref, pos_ref, coeff_ref, tc, fit, turned, payload, arrived, keys_out, keys_in, gath, weights, total,
+    small_sem, tc_sem, fit_sem, key_send, key_recv, pay_send, pay_recv,
     x_send, x_recv, sib_send, sib_recv, fwd_send, fwd_recv,
 ):
     me = lax.axis_index("mu")
@@ -48,6 +49,14 @@
             tc_hbm.at[:, :, columns], tc.at[:, :, columns], tc_sem.at[c]
         )
 
+    small = [
+        pltpu.make_async_copy(source, target, small_sem.at[i])
+        for i, (source, target) in enumerate((
+            (mu_hbm, mu_ref), (site_hbm, site_ref), (pos_hbm, pos_ref), (coeff_hbm, coeff_ref),
+        ))
+    ]
+    for copy in small:
+        copy.start()
     for c in range(CHUNKS):
         tc_copy(c).start()
     site = lax.rem(me, SITES)
@@ -68,6 +77,8 @@
     for peer in (sibling, across, diagonal):
         pl.semaphore_signal(barrier, inc=1, device_id={"pa": peer}, device_id_type=MESH)
 
+    for copy in small:
+        copy.wait()
     slots = []
     for t in range(pairs):
         rank = jnp.int32(0)
@@ -78,8 +89,12 @@
     table = jnp.full((SLOTS, LANES), -1.0, F32)
     for t in range(pairs):
         table = jnp.where(key_row == slots[t], pos_ref[0, t].astype(F32), table)
-    keys_out[...] = table
-    keys_in[0] = table
+    first_half = lax.broadcasted_iota(jnp.int32, (1, LANES), 1) < block
+    for s in range(SITES):
+        keys_out[s] = jnp.where(
+            first_half, table[s * CAP:s * CAP + 1, :], table[s * CAP + 1:s * CAP + 2, :]
+        )
+    keys_in[0] = keys_out[site]
     slot_row = lax.broadcasted_iota(jnp.int32, (groups, SLOTS, LANES), 1).reshape(
         groups * SLOTS, LANES
     )
@@ -102,7 +117,7 @@
 
     def key_copy(d):
         return pltpu.make_async_remote_copy(
-            src_ref=keys_out, dst_ref=keys_in.at[d],
+            src_ref=keys_out.at[lax.rem(lax.rem(me + d, n), SITES)], dst_ref=keys_in.at[d],
             send_sem=key_send.at[d], recv_sem=key_recv.at[d],
             device_id={"mu": lax.rem(me + d, n)}, device_id_type=MESH,
         )
@@ -192,11 +207,11 @@
 
     for c in range(CHUNKS):
         def add_source(d, sums, c=c):
-            if n > 16 or d:
-                pass
             sums = list(sums)
+            both = keys_in[d]
+            other = pltpu.roll(both, block, 1)
             for cap in range(CAP):
-                key = keys_in[d, pl.ds(site * CAP + cap, 1), :]
+                key = jnp.where(first_half, *((both, other) if cap == 0 else (other, both)))
                 value = arrived[c, d, cap * rows:(cap + 1) * rows, :].astype(F32)
                 for k in range(NU_SITE):
                     sums[k] = sums[k] + jnp.where(key == float(k), value, 0.0)
@@ -251,33 +266,36 @@
     shards = lax.axis_size("pa")
     rows = columns // CHUNKS // LANES
     pair_blocks = coeff.reshape(coeff.shape[0] // LANES, LANES, orbitals).transpose(0, 2, 1)
-    smem = pl.BlockSpec(memory_space=pltpu.SMEM)
     vmem = pl.BlockSpec(memory_space=pltpu.VMEM)
     hbm = pl.BlockSpec(memory_space=pltpu.HBM)
     dma = pltpu.SemaphoreType.DMA
     result = pl.pallas_call(
         functools.partial(kernel, n),
         out_shape=jax.ShapeDtypeStruct((NU_SITE, columns // LANES, LANES), BF16),
-        in_specs=[smem, smem, smem, vmem, hbm, hbm],
+        in_specs=[hbm] * 6,
         out_specs=vmem,
         scratch_shapes=[
+            pltpu.SMEM((1, pairs), jnp.int32),
+            pltpu.SMEM((1, pairs), jnp.int32),
+            pltpu.SMEM((1, pairs), jnp.int32),
+            pltpu.VMEM(pair_blocks.shape, BF16),
             pltpu.VMEM((pairs, block, columns), BF16),
             pltpu.VMEM((NU_SITE,) + fitting.shape[1:], BF16),
             pltpu.VMEM((n * CAP * rows, LANES), F32),
             pltpu.VMEM((CHUNKS, n, CAP * rows, LANES), BF16),
             pltpu.VMEM((CHUNKS, n, CAP * rows, LANES), BF16),
-            pltpu.VMEM((SLOTS, LANES), F32),
-            pltpu.VMEM((n, SLOTS, LANES), F32),
+            pltpu.VMEM((SITES, 1, LANES), F32),
+            pltpu.VMEM((n, 1, LANES), F32),
             pltpu.VMEM((CHUNKS, shards, NU_SITE, rows, LANES), BF16),
             pltpu.VMEM((NU_SITE, shards, 2 * block, LANES), BF16),
             pltpu.VMEM((NU_SITE, columns // LANES, LANES), F32),
-            dma((CHUNKS,)), dma,
+            dma((4,)), dma((CHUNKS,)), dma,
             dma((n,)), dma((n,)), dma((CHUNKS, n)), dma((CHUNKS, n)),
             dma((CHUNKS,)), dma((CHUNKS,)), dma((CHUNKS,)),
             dma((CHUNKS,)), dma((CHUNKS,)), dma((CHUNKS,)),
         ],
         compiler_params=pltpu.CompilerParams(
-            collective_id=0, has_side_effects=True, vmem_limit_bytes=40 * 1024 * 1024
+            collective_id=0, has_side_effects=True, vmem_limit_bytes=VMEM_BYTES
         ),
     )(pair_mu, pair_site[:, :, 0], pair_pos, pair_blocks, three_center, fitting)
     shape = (NU_SITE, CHUNKS * rows * LANES)

time: 23.3 us -> 18.9 us (0.81)
  local copies, waits for them, and re-layouts: 6.55 us -> 1.63 us
  Pallas kernels: 16.5 us -> 17.1 us
    unnamed x12 -> x0, local copies, waits for them, and re-layouts: 5.82 us -> none
    reshape x1, local copies, waits for them, and re-layouts: 0.74 us -> 1.63 us  [local(): return result.reshape((1, NU_SITE, 1, shape[1]))]
    pallas_call x1, Pallas kernels: 16.5 us -> 17.1 us  [local(): pl.pallas_call(functools.partial(kernel, n), out_shape=jax.ShapeDtypeStru...]
where the time goes in v2:
time: 18.9 us; the launch traced here: 18.8 us
  Pallas kernels  17.1 us (90%)
  local copies, waits for them, and re-layouts  1.63 us (9%)
    pallas_call x1, Pallas kernels, local(): pl.pallas_call(functools.partial(kernel, n), out_shape=jax.ShapeDtypeStru...  17.1 us
    reshape x1, local copies, waits for them, and re-layouts, local(): return result.reshape((1, NU_SITE, 1, shape[1]))  1.63 us

profile of v2, /device:TPU:1, one launch (start us, length us, event | category | flops | bytes accessed | tf_op | source)
XLA Modules:
  0.0 18.8 jit_solution(5721293577210196841)
XLA Ops:
  0.0 17.1 %shard_map.64 = bf16[12,32,128]{2,1,0:T(8,128)(2,1)} custom-call(s32[1,5]{1,0:T(1,128)} %mu_hbm.1, s32[1,5]{1,0:T(1,128)} %bitcast.5, s32[1,5]{1,0:T(1,128)} %pos_hbm.1, bf16[24,2,128]{2,1,0:T(2,128)(2,1)} %bitcast.4, bf16[5,64,4096]{2,1,0:T(8,128)(2,1)} %tc_hbm.1, bf16[48,64,256]{2,1,0:T(8,128)(2,1)} %fit_hbm.1), custom_call_target="tpu_custom_call" | custom-call | tf_op jit(solution)/shard_map/pallas_call | solution.py:272
  17.2 1.6 %reshape.7 = bf16[1,12,1,4096]{3,1,2,0:T(8,128)(2,1)} reshape(bf16[12,32,128]{2,1,0:T(8,128)(2,1)} %shard_map.64) | data formatting | bytes 196608 | tf_op jit(solution)/shard_map/reshape | solution.py:302

commit v3 on v2

--- a/solution.py
+++ b/solution.py
@@ -29,7 +29,7 @@
 
 def kernel(
     n, mu_hbm, site_hbm, pos_hbm, coeff_hbm, tc_hbm, fit_hbm, out_ref,
-    mu_ref, site_ref, pos_ref, coeff_ref, tc, fit, turned, payload, arrived, keys_out, keys_in, gath, weights, total,
+    mu_ref, site_ref, pos_ref, coeff_ref, tc, fit, turned, payload, arrived, keys_out, keys_in, gath, weights, total, spread,
     small_sem, tc_sem, fit_sem, key_send, key_recv, pay_send, pay_recv,
     x_send, x_recv, sib_send, sib_recv, fwd_send, fwd_recv,
 ):
@@ -227,29 +227,36 @@
             each_peer(lambda d, c=c: pay_copy(c, d).wait_recv())
             sums = lax.fori_loop(0, n, add_source, sums)
         for k in range(NU_SITE):
-            gath[c, shard, k] = sums[k].astype(BF16)
+            gath[c, shard, k * rows:(k + 1) * rows, :] = sums[k].astype(BF16)
         x_copy(c).start()
         sib_copy(c).start()
 
-    def product(k, chip):
-        lines = [
-            jnp.concatenate([gath[c, 2 * chip, k], gath[c, 2 * chip + 1, k]], axis=1)
-            for c in range(CHUNKS)
-        ]
-        held = weights[k, pl.ds(2 * chip, 2)].reshape(4 * block, LANES)
-        return jnp.dot(jnp.concatenate(lines, axis=0), held, preferred_element_type=F32)
-
-    chip = lax.div(shard, 2)
+    def lines(k, which):
+        return jnp.concatenate(
+            [gath[c, which, k * rows:(k + 1) * rows, :] for c in range(CHUNKS)], axis=0
+        )
+
+    def product(k, which):
+        return jnp.dot(lines(k, which), weights[k, which], preferred_element_type=F32)
+
+    for c in range(CHUNKS):
+        sib_copy(c).wait_recv()
+    first = 2 * lax.div(shard, 2)
+    for k in range(NU_SITE):
+        pair = jnp.concatenate([lines(k, first), lines(k, first + 1)], axis=1)
+        held = weights[k, pl.ds(first, 2)].reshape(4 * block, LANES)
+        total[k] = jnp.dot(pair, held, preferred_element_type=F32)
     for c in range(CHUNKS):
         x_copy(c).wait_recv()
         fwd_copy(c).start()
-        sib_copy(c).wait_recv()
     for k in range(NU_SITE):
-        total[k] = product(k, chip)
+        total[k] += product(k, across)
     for c in range(CHUNKS):
         fwd_copy(c).wait_recv()
     for k in range(NU_SITE):
-        out_ref[k] = (total[k] + product(k, 1 - chip)).astype(BF16)
+        spread[pl.ds(k, CHUNKS * rows, stride=16), :] = total[k] + product(k, diagonal)
+    for j in range(CHUNKS * rows):
+        out_ref[:, j * LANES:(j + 1) * LANES] = spread[j * 16:j * 16 + NU_SITE, :].astype(BF16)
 
     each_peer(lambda d: key_copy(d).wait_send())
     for c in range(CHUNKS):
@@ -271,7 +278,7 @@
     dma = pltpu.SemaphoreType.DMA
     result = pl.pallas_call(
         functools.partial(kernel, n),
-        out_shape=jax.ShapeDtypeStruct((NU_SITE, columns // LANES, LANES), BF16),
+        out_shape=jax.ShapeDtypeStruct((NU_SITE, columns), BF16),
         in_specs=[hbm] * 6,
         out_specs=vmem,
         scratch_shapes=[
@@ -286,9 +293,10 @@
             pltpu.VMEM((CHUNKS, n, CAP * rows, LANES), BF16),
             pltpu.VMEM((SITES, 1, LANES), F32),
             pltpu.VMEM((n, 1, LANES), F32),
-            pltpu.VMEM((CHUNKS, shards, NU_SITE, rows, LANES), BF16),
+            pltpu.VMEM((CHUNKS, shards, NU_SITE * rows, LANES), BF16),
             pltpu.VMEM((NU_SITE, shards, 2 * block, LANES), BF16),
             pltpu.VMEM((NU_SITE, columns // LANES, LANES), F32),
+            pltpu.VMEM((columns // LANES * 16, LANES), F32),
             dma((4,)), dma((CHUNKS,)), dma,
             dma((n,)), dma((n,)), dma((CHUNKS, n)), dma((CHUNKS, n)),
             dma((CHUNKS,)), dma((CHUNKS,)), dma((CHUNKS,)),
@@ -298,8 +306,7 @@
             collective_id=0, has_side_effects=True, vmem_limit_bytes=VMEM_BYTES
         ),
     )(pair_mu, pair_site[:, :, 0], pair_pos, pair_blocks, three_center, fitting)
-    shape = (NU_SITE, CHUNKS * rows * LANES)
-    return result.reshape((1, NU_SITE, 1, shape[1]))
+    return result.reshape((1, NU_SITE, 1, columns))
 
 
 def solution(mesh):

time: 18.9 us -> 18.9 us (level)
    reshape x1 -> x0, local copies, waits for them, and re-layouts: 1.63 us -> none  [local(): return result.reshape((1, NU_SITE, 1, shape[1]))]
    unnamed x0 -> x1, local copies, waits for them, and re-layouts: none -> 1.57 us
where the time goes in v3:
time: 18.9 us; the launch traced here: 18.7 us
  Pallas kernels  17.2 us (91%)
  local copies, waits for them, and re-layouts  1.57 us (8%)
    pallas_call x1, Pallas kernels, local(): pl.pallas_call(functools.partial(kernel, n), out_shape=jax.ShapeDtypeStru...  17.2 us
    unnamed x1, local copies, waits for them, and re-layouts  1.57 us

profile of v3, /device:TPU:1, one launch (start us, length us, event | category | flops | bytes accessed | tf_op | source)
XLA Modules:
  0.0 18.7 jit_solution(14558892272874056243)
XLA Ops:
  0.0 17.2 %shard_map.64 = bf16[12,4096]{1,0:T(8,128)(2,1)} custom-call(s32[1,5]{1,0:T(1,128)} %mu_hbm.1, s32[1,5]{1,0:T(1,128)} %bitcast.7, s32[1,5]{1,0:T(1,128)} %pos_hbm.1, bf16[24,2,128]{2,1,0:T(2,128)(2,1)} %bitcast.6, bf16[5,64,4096]{2,1,0:T(8,128)(2,1)} %tc_hbm.1, bf16[48,64,256]{2,1,0:T(8,128)(2,1)} %fit_hbm.1), custom_call_target="tpu_custom_call" | custom-call | tf_op jit(solution)/shard_map/pallas_call | solution.py:279
  17.2 1.6 %copy.8 = bf16[1,12,1,4096]{3,1,2,0:T(8,128)(2,1)} copy(bf16[1,12,1,4096]{3,1,2,0:T(8,128)(2,1)} %bitcast.5) | data formatting | bytes 196608

commit v4 on v3

--- a/solution.py
+++ b/solution.py
@@ -13,7 +13,7 @@
 SLOTS = SITES * CAP
 LANES = 128
 CHUNKS = 2
-VMEM_BYTES = 60 * 1000000
+VMEM_BYTES = 40 * 1024 * 1024
 MESH = pl.DeviceIdType.MESH
 F32 = jnp.float32
 BF16 = jnp.bfloat16
@@ -305,7 +305,12 @@
         compiler_params=pltpu.CompilerParams(
             collective_id=0, has_side_effects=True, vmem_limit_bytes=VMEM_BYTES
         ),
-    )(pair_mu, pair_site[:, :, 0], pair_pos, pair_blocks, three_center, fitting)
+    )(*(
+        pltpu.with_memory_space_constraint(operand, pltpu.HBM)
+        for operand in (
+            pair_mu, pair_site[:, :, 0], pair_pos, pair_blocks, three_center, fitting
+        )
+    ))
     return result.reshape((1, NU_SITE, 1, columns))
 
 

time: 18.9 us -> 17.3 us (0.915)
  local copies, waits for them, and re-layouts: 1.57 us -> 0.66 us
  Pallas kernels: 17.2 us -> 16.5 us
    unnamed x1, local copies, waits for them, and re-layouts: 1.57 us -> 0.66 us
    pallas_call x1, Pallas kernels: 17.2 us -> 16.5 us  [local(): pl.pallas_call(functools.partial(kernel, n), out_shape=jax.ShapeDtypeStru...]
where the time goes in v4:
time: 17.3 us; the launch traced here: 17.2 us
  Pallas kernels  16.5 us (95%)
  local copies, waits for them, and re-layouts  0.66 us (4%)
    pallas_call x1, Pallas kernels, local(): pl.pallas_call(functools.partial(kernel, n), out_shape=jax.ShapeDtypeStru...  16.5 us
    unnamed x1, local copies, waits for them, and re-layouts  0.66 us

profile of v4, /device:TPU:1, one launch (start us, length us, event | category | flops | bytes accessed | tf_op | source)
XLA Modules:
  0.0 17.2 jit_solution(9798430125479841701)
XLA Ops:
  0.0 16.5 %shard_map.64 = bf16[12,4096]{1,0:T(8,128)(2,1)S(1)} custom-call(s32[1,5]{1,0:T(1,128)} %mu_hbm.1, s32[1,5]{1,0:T(1,128)} %bitcast.7, s32[1,5]{1,0:T(1,128)} %pos_hbm.1, bf16[24,2,128]{2,1,0:T(2,128)(2,1)} %bitcast.6, bf16[5,64,4096]{2,1,0:T(8,128)(2,1)} %tc_hbm.1, bf16[48,64,256]{2,1,0:T(8,128)(2,1)} %fit_hbm.1), custom_call_target="tpu_custom_call" | custom-call | tf_op jit(solution)/shard_map/pallas_call | solution.py:279
  16.5 0.7 %copy.8 = bf16[1,12,1,4096]{3,1,2,0:T(8,128)(2,1)} copy(bf16[1,12,1,4096]{3,1,2,0:T(8,128)(2,1)S(1)} %bitcast.5) | data formatting | bytes 196608

commit v5 on v4

--- a/solution.py
+++ b/solution.py
@@ -29,7 +29,7 @@
 
 def kernel(
     n, mu_hbm, site_hbm, pos_hbm, coeff_hbm, tc_hbm, fit_hbm, out_ref,
-    mu_ref, site_ref, pos_ref, coeff_ref, tc, fit, turned, payload, arrived, keys_out, keys_in, gath, weights, total, spread,
+    mu_ref, site_ref, pos_ref, coeff_ref, tc, fit, turned, payload, arrived, keys_out, keys_in, gath, total, spread,
     small_sem, tc_sem, fit_sem, key_send, key_recv, pay_send, pay_recv,
     x_send, x_recv, sib_send, sib_recv, fwd_send, fwd_recv,
 ):
@@ -43,6 +43,18 @@
     rows = width // LANES
     groups = coeff_ref.shape[1]
 
+    barrier = pltpu.get_barrier_semaphore()
+
+    def greet(d, carry):
+        pl.semaphore_signal(
+            barrier, inc=1, device_id={"mu": lax.rem(me + d + 1, n)}, device_id_type=MESH
+        )
+        return carry
+
+    loop(n - 1, greet, 0)
+    for peer in (sibling, across, diagonal):
+        pl.semaphore_signal(barrier, inc=1, device_id={"pa": peer}, device_id_type=MESH)
+
     def tc_copy(c):
         columns = pl.ds(c * width, width)
         return pltpu.make_async_copy(
@@ -64,18 +76,6 @@
         fit_hbm.at[pl.ds(site * NU_SITE, NU_SITE)], fit, fit_sem
     )
     fit_copy.start()
-
-    barrier = pltpu.get_barrier_semaphore()
-
-    def greet(d, carry):
-        pl.semaphore_signal(
-            barrier, inc=1, device_id={"mu": lax.rem(me + d + 1, n)}, device_id_type=MESH
-        )
-        return carry
-
-    loop(n - 1, greet, 0)
-    for peer in (sibling, across, diagonal):
-        pl.semaphore_signal(barrier, inc=1, device_id={"pa": peer}, device_id_type=MESH)
 
     for copy in small:
         copy.wait()
@@ -176,17 +176,6 @@
             each_peer(lambda d: key_copy(d).start())
         each_peer(lambda d, c=c: pay_copy(c, d).start())
 
-    fit_copy.wait()
-    for k in range(NU_SITE):
-        double = jnp.concatenate([fit[k], fit[k]], axis=0)
-        flipped = double.T
-        lane_w = lax.broadcasted_iota(jnp.int32, (block, 2 * block), 1)
-        for q in range(4):
-            piece = flipped[q * block:(q + 1) * block, :]
-            zero = jnp.zeros_like(piece)
-            weights[k, q, 0:block, :] = jnp.where(lane_w < block, piece, zero)
-            weights[k, q, block:2 * block, :] = jnp.where(lane_w < block, zero, piece)
-
     each_peer(lambda d: key_copy(d).wait_recv())
 
     def pa_copy(c, which, target, send, recv):
@@ -236,25 +225,32 @@
             [gath[c, which, k * rows:(k + 1) * rows, :] for c in range(CHUNKS)], axis=0
         )
 
-    def product(k, which):
-        return jnp.dot(lines(k, which), weights[k, which], preferred_element_type=F32)
-
+    fit_copy.wait()
+    half_lane = lax.broadcasted_iota(jnp.int32, (CHUNKS * rows, LANES), 1) < block
+
+    def product(k, chip):
+        low, high = lines(k, 2 * chip), lines(k, 2 * chip + 1)
+        even = jnp.where(half_lane, low, pltpu.roll(high, block, 1))
+        odd = jnp.where(half_lane, pltpu.roll(low, block, 1), high)
+        held = fit[k, :, pl.ds(pl.multiple_of(chip * LANES, LANES), LANES)]
+        both = lax.dot_general(
+            jnp.concatenate([even, odd], axis=0), jnp.concatenate([held, held], axis=0),
+            (((1,), (1,)), ((), ())), preferred_element_type=F32,
+        )
+        return jnp.where(half_lane, both[:CHUNKS * rows], both[CHUNKS * rows:])
+
+    chip = lax.div(shard, 2)
     for c in range(CHUNKS):
         sib_copy(c).wait_recv()
-    first = 2 * lax.div(shard, 2)
     for k in range(NU_SITE):
-        pair = jnp.concatenate([lines(k, first), lines(k, first + 1)], axis=1)
-        held = weights[k, pl.ds(first, 2)].reshape(4 * block, LANES)
-        total[k] = jnp.dot(pair, held, preferred_element_type=F32)
+        total[k] = product(k, chip)
     for c in range(CHUNKS):
         x_copy(c).wait_recv()
         fwd_copy(c).start()
-    for k in range(NU_SITE):
-        total[k] += product(k, across)
     for c in range(CHUNKS):
         fwd_copy(c).wait_recv()
     for k in range(NU_SITE):
-        spread[pl.ds(k, CHUNKS * rows, stride=16), :] = total[k] + product(k, diagonal)
+        spread[pl.ds(k, CHUNKS * rows, stride=16), :] = total[k] + product(k, 1 - chip)
     for j in range(CHUNKS * rows):
         out_ref[:, j * LANES:(j + 1) * LANES] = spread[j * 16:j * 16 + NU_SITE, :].astype(BF16)
 
@@ -294,7 +290,6 @@
             pltpu.VMEM((SITES, 1, LANES), F32),
             pltpu.VMEM((n, 1, LANES), F32),
             pltpu.VMEM((CHUNKS, shards, NU_SITE * rows, LANES), BF16),
-            pltpu.VMEM((NU_SITE, shards, 2 * block, LANES), BF16),
             pltpu.VMEM((NU_SITE, columns // LANES, LANES), F32),
             pltpu.VMEM((columns // LANES * 16, LANES), F32),
             dma((4,)), dma((CHUNKS,)), dma,

time: 17.3 us -> 17.5 us (1.012)
  Pallas kernels: 16.5 us -> 16.7 us
    pallas_call x1, Pallas kernels: 16.5 us -> 16.7 us  [local(): pl.pallas_call(functools.partial(kernel, n), out_shape=jax.ShapeDtypeStru...]
where the time goes in v5:
time: 17.5 us; the launch traced here: 17.4 us
  Pallas kernels  16.7 us (95%)
  local copies, waits for them, and re-layouts  0.66 us (4%)
    pallas_call x1, Pallas kernels, local(): pl.pallas_call(functools.partial(kernel, n), out_shape=jax.ShapeDtypeStru...  16.7 us
    unnamed x1, local copies, waits for them, and re-layouts  0.66 us

profile of v5, /device:TPU:1, one launch (start us, length us, event | category | flops | bytes accessed | tf_op | source)
XLA Modules:
  0.0 17.4 jit_solution(7179950841878202603)
XLA Ops:
  0.0 16.7 %shard_map.64 = bf16[12,4096]{1,0:T(8,128)(2,1)S(1)} custom-call(s32[1,5]{1,0:T(1,128)} %mu_hbm.1, s32[1,5]{1,0:T(1,128)} %bitcast.7, s32[1,5]{1,0:T(1,128)} %pos_hbm.1, bf16[24,2,128]{2,1,0:T(2,128)(2,1)} %bitcast.6, bf16[5,64,4096]{2,1,0:T(8,128)(2,1)} %tc_hbm.1, bf16[48,64,256]{2,1,0:T(8,128)(2,1)} %fit_hbm.1), custom_call_target="tpu_custom_call" | custom-call | tf_op jit(solution)/shard_map/pallas_call | solution.py:275
  16.7 0.7 %copy.8 = bf16[1,12,1,4096]{3,1,2,0:T(8,128)(2,1)} copy(bf16[1,12,1,4096]{3,1,2,0:T(8,128)(2,1)S(1)} %bitcast.5) | data formatting | bytes 196608

commit v6 on v5

--- a/solution.py
+++ b/solution.py
@@ -12,7 +12,8 @@
 CAP = 2
 SLOTS = SITES * CAP
 LANES = 128
-CHUNKS = 2
+CHUNKS = 4
+LAG = 2
 VMEM_BYTES = 40 * 1024 * 1024
 MESH = pl.DeviceIdType.MESH
 F32 = jnp.float32
@@ -219,6 +220,9 @@
             gath[c, shard, k * rows:(k + 1) * rows, :] = sums[k].astype(BF16)
         x_copy(c).start()
         sib_copy(c).start()
+        if c >= LAG:
+            x_copy(c - LAG).wait_recv()
+            fwd_copy(c - LAG).start()
 
     def lines(k, which):
         return jnp.concatenate(
@@ -244,7 +248,7 @@
         sib_copy(c).wait_recv()
     for k in range(NU_SITE):
         total[k] = product(k, chip)
-    for c in range(CHUNKS):
+    for c in range(CHUNKS - LAG, CHUNKS):
         x_copy(c).wait_recv()
         fwd_copy(c).start()
     for c in range(CHUNKS):

time: 17.5 us -> 19.7 us (1.13)
  Pallas kernels: 16.7 us -> 18.9 us
    pallas_call x1, Pallas kernels: 16.7 us -> 18.9 us  [local(): pl.pallas_call(functools.partial(kernel, n), out_shape=jax.ShapeDtypeStru...]
where the time goes in v6:
time: 19.7 us; the launch traced here: 19.6 us
  Pallas kernels  18.9 us (96%)
  local copies, waits for them, and re-layouts  0.66 us (3%)
    pallas_call x1, Pallas kernels, local(): pl.pallas_call(functools.partial(kernel, n), out_shape=jax.ShapeDtypeStru...  18.9 us
    unnamed x1, local copies, waits for them, and re-layouts  0.66 us

profile of v6, /device:TPU:1, one launch (start us, length us, event | category | flops | bytes accessed | tf_op | source)
XLA Modules:
  0.0 19.6 jit_solution(855753265264767813)
XLA Ops:
  0.0 18.9 %shard_map.64 = bf16[12,4096]{1,0:T(8,128)(2,1)S(1)} custom-call(s32[1,5]{1,0:T(1,128)} %mu_hbm.1, s32[1,5]{1,0:T(1,128)} %bitcast.7, s32[1,5]{1,0:T(1,128)} %pos_hbm.1, bf16[24,2,128]{2,1,0:T(2,128)(2,1)} %bitcast.6, bf16[5,64,4096]{2,1,0:T(8,128)(2,1)} %tc_hbm.1, bf16[48,64,256]{2,1,0:T(8,128)(2,1)} %fit_hbm.1), custom_call_target="tpu_custom_call" | custom-call | tf_op jit(solution)/shard_map/pallas_call | solution.py:279
  18.9 0.7 %copy.8 = bf16[1,12,1,4096]{3,1,2,0:T(8,128)(2,1)} copy(bf16[1,12,1,4096]{3,1,2,0:T(8,128)(2,1)S(1)} %bitcast.5) | data formatting | bytes 196608

commit v7 on v5

--- a/solution.py
+++ b/solution.py
@@ -13,6 +13,8 @@
 SLOTS = SITES * CAP
 LANES = 128
 CHUNKS = 2
+PARTS = 2
+HELD = NU_SITE // PARTS
 VMEM_BYTES = 40 * 1024 * 1024
 MESH = pl.DeviceIdType.MESH
 F32 = jnp.float32
@@ -40,7 +42,7 @@
     diagonal = lax.rem(sibling + 2, 4)
     pairs, block, _ = tc.shape
     width = tc.shape[2] // CHUNKS
-    rows = width // LANES
+    rows = tc.shape[2] // LANES
     groups = coeff_ref.shape[1]
 
     barrier = pltpu.get_barrier_semaphore()
@@ -122,18 +124,18 @@
             device_id={"mu": lax.rem(me + d, n)}, device_id_type=MESH,
         )
 
-    def pay_copy(c, d):
+    def pay_copy(d):
         owner = lax.rem(me + d, n)
         return pltpu.make_async_remote_copy(
-            src_ref=payload.at[c, owner], dst_ref=arrived.at[c, d],
-            send_sem=pay_send.at[c, d], recv_sem=pay_recv.at[c, d],
+            src_ref=payload.at[owner], dst_ref=arrived.at[d],
+            send_sem=pay_send.at[d], recv_sem=pay_recv.at[d],
             device_id={"mu": owner}, device_id_type=MESH,
         )
 
-    def make_payload(c):
+    def transform(c):
         tc_copy(c).wait()
-        for j in range(0, rows, 2):
-            start = c * width + j * LANES
+        for j in range(c * width // LANES, (c + 1) * width // LANES, 2):
+            start = j * LANES
             acc = None
             for t, part in zip(range(0, pairs, 2), left):
                 depth = part.shape[1]
@@ -145,16 +147,6 @@
             turned[pl.ds(j, n * CAP, stride=rows), :] = acc[:, :LANES]
             turned[pl.ds(j + 1, n * CAP, stride=rows), :] = acc[:, LANES:]
 
-        def pack(w, carry):
-            first = w * CAP * rows
-            if not isinstance(w, int):
-                first = pl.multiple_of(first, CAP * rows)
-            payload[c, w] = turned[pl.ds(first, CAP * rows), :].astype(BF16)
-            return carry
-
-        loop(n, pack, 0)
-        arrived[c, 0] = payload[c, me]
-
     order = list(range(1, n))
     if n <= 16:
         order.sort(key=lambda d: abs(d - n // 2))
@@ -169,12 +161,21 @@
                 return carry
             lax.fori_loop(1, n, body, 0)
 
+    pl.semaphore_wait(barrier, n - 1 + 3)
+    each_peer(lambda d: key_copy(d).start())
     for c in range(CHUNKS):
-        make_payload(c)
-        if c == 0:
-            pl.semaphore_wait(barrier, n - 1 + 3)
-            each_peer(lambda d: key_copy(d).start())
-        each_peer(lambda d, c=c: pay_copy(c, d).start())
+        transform(c)
+
+    def pack(w, carry):
+        first = w * CAP * rows
+        if not isinstance(w, int):
+            first = pl.multiple_of(first, CAP * rows)
+        payload[w] = turned[pl.ds(first, CAP * rows), :].astype(BF16)
+        return carry
+
+    loop(n, pack, 0)
+    each_peer(lambda d: pay_copy(d).start())
+    arrived[0] = payload[me]
 
     each_peer(lambda d: key_copy(d).wait_recv())
 
@@ -194,69 +195,68 @@
     def fwd_copy(c):
         return pa_copy(c, across, sibling, fwd_send, fwd_recv)
 
-    for c in range(CHUNKS):
+    for c in range(PARTS):
         def add_source(d, sums, c=c):
             sums = list(sums)
             both = keys_in[d]
             other = pltpu.roll(both, block, 1)
             for cap in range(CAP):
                 key = jnp.where(first_half, *((both, other) if cap == 0 else (other, both)))
-                value = arrived[c, d, cap * rows:(cap + 1) * rows, :].astype(F32)
-                for k in range(NU_SITE):
-                    sums[k] = sums[k] + jnp.where(key == float(k), value, 0.0)
+                value = arrived[d, cap * rows:(cap + 1) * rows, :].astype(F32)
+                for k in range(HELD):
+                    sums[k] = sums[k] + jnp.where(key == float(c * HELD + k), value, 0.0)
             return tuple(sums)
 
-        sums = tuple(jnp.zeros((rows, LANES), F32) for _ in range(NU_SITE))
+        sums = tuple(jnp.zeros((rows, LANES), F32) for _ in range(HELD))
         if n <= 16:
             sums = add_source(0, sums)
             for d in reversed(order):
-                pay_copy(c, d).wait_recv()
+                if c == 0:
+                    pay_copy(d).wait_recv()
                 sums = add_source(d, sums)
         else:
-            each_peer(lambda d, c=c: pay_copy(c, d).wait_recv())
+            if c == 0:
+                each_peer(lambda d: pay_copy(d).wait_recv())
             sums = lax.fori_loop(0, n, add_source, sums)
-        for k in range(NU_SITE):
+        for k in range(HELD):
             gath[c, shard, k * rows:(k + 1) * rows, :] = sums[k].astype(BF16)
         x_copy(c).start()
         sib_copy(c).start()
 
-    def lines(k, which):
-        return jnp.concatenate(
-            [gath[c, which, k * rows:(k + 1) * rows, :] for c in range(CHUNKS)], axis=0
-        )
-
     fit_copy.wait()
-    half_lane = lax.broadcasted_iota(jnp.int32, (CHUNKS * rows, LANES), 1) < block
-
-    def product(k, chip):
-        low, high = lines(k, 2 * chip), lines(k, 2 * chip + 1)
+    half_lane = lax.broadcasted_iota(jnp.int32, (rows, LANES), 1) < block
+
+    def product(c, k, chip):
+        low = gath[c, 2 * chip, k * rows:(k + 1) * rows, :]
+        high = gath[c, 2 * chip + 1, k * rows:(k + 1) * rows, :]
         even = jnp.where(half_lane, low, pltpu.roll(high, block, 1))
         odd = jnp.where(half_lane, pltpu.roll(low, block, 1), high)
-        held = fit[k, :, pl.ds(pl.multiple_of(chip * LANES, LANES), LANES)]
+        held = fit[c * HELD + k, :, pl.ds(pl.multiple_of(chip * LANES, LANES), LANES)]
         both = lax.dot_general(
             jnp.concatenate([even, odd], axis=0), jnp.concatenate([held, held], axis=0),
             (((1,), (1,)), ((), ())), preferred_element_type=F32,
         )
-        return jnp.where(half_lane, both[:CHUNKS * rows], both[CHUNKS * rows:])
+        return jnp.where(half_lane, both[:rows], both[rows:])
 
     chip = lax.div(shard, 2)
-    for c in range(CHUNKS):
+    for c in range(PARTS):
         sib_copy(c).wait_recv()
-    for k in range(NU_SITE):
-        total[k] = product(k, chip)
-    for c in range(CHUNKS):
+        for k in range(HELD):
+            total[c * HELD + k] = product(c, k, chip)
+    for c in range(PARTS):
         x_copy(c).wait_recv()
         fwd_copy(c).start()
-    for c in range(CHUNKS):
+    for c in range(PARTS):
         fwd_copy(c).wait_recv()
-    for k in range(NU_SITE):
-        spread[pl.ds(k, CHUNKS * rows, stride=16), :] = total[k] + product(k, 1 - chip)
-    for j in range(CHUNKS * rows):
+        for k in range(HELD):
+            at = c * HELD + k
+            spread[pl.ds(at, rows, stride=16), :] = total[at] + product(c, k, 1 - chip)
+    for j in range(rows):
         out_ref[:, j * LANES:(j + 1) * LANES] = spread[j * 16:j * 16 + NU_SITE, :].astype(BF16)
 
     each_peer(lambda d: key_copy(d).wait_send())
-    for c in range(CHUNKS):
-        each_peer(lambda d, c=c: pay_copy(c, d).wait_send())
+    each_peer(lambda d: pay_copy(d).wait_send())
+    for c in range(PARTS):
         x_copy(c).wait_send()
         sib_copy(c).wait_send()
         fwd_copy(c).wait_send()
@@ -267,7 +267,7 @@
     pairs, block, columns = three_center.shape
     orbitals = coeff.shape[1]
     shards = lax.axis_size("pa")
-    rows = columns // CHUNKS // LANES
+    rows = columns // LANES
     pair_blocks = coeff.reshape(coeff.shape[0] // LANES, LANES, orbitals).transpose(0, 2, 1)
     vmem = pl.BlockSpec(memory_space=pltpu.VMEM)
     hbm = pl.BlockSpec(memory_space=pltpu.HBM)
@@ -285,17 +285,17 @@
             pltpu.VMEM((pairs, block, columns), BF16),
             pltpu.VMEM((NU_SITE,) + fitting.shape[1:], BF16),
             pltpu.VMEM((n * CAP * rows, LANES), F32),
-            pltpu.VMEM((CHUNKS, n, CAP * rows, LANES), BF16),
-            pltpu.VMEM((CHUNKS, n, CAP * rows, LANES), BF16),
+            pltpu.VMEM((n, CAP * rows, LANES), BF16),
+            pltpu.VMEM((n, CAP * rows, LANES), BF16),
             pltpu.VMEM((SITES, 1, LANES), F32),
             pltpu.VMEM((n, 1, LANES), F32),
-            pltpu.VMEM((CHUNKS, shards, NU_SITE * rows, LANES), BF16),
+            pltpu.VMEM((PARTS, shards, HELD * rows, LANES), BF16),
             pltpu.VMEM((NU_SITE, columns // LANES, LANES), F32),
             pltpu.VMEM((columns // LANES * 16, LANES), F32),
             dma((4,)), dma((CHUNKS,)), dma,
-            dma((n,)), dma((n,)), dma((CHUNKS, n)), dma((CHUNKS, n)),
-            dma((CHUNKS,)), dma((CHUNKS,)), dma((CHUNKS,)),
-            dma((CHUNKS,)), dma((CHUNKS,)), dma((CHUNKS,)),
+            dma((n,)), dma((n,)), dma((n,)), dma((n,)),
+            dma((PARTS,)), dma((PARTS,)), dma((PARTS,)),
+            dma((PARTS,)), dma((PARTS,)), dma((PARTS,)),
         ],
         compiler_params=pltpu.CompilerParams(
             collective_id=0, has_side_effects=True, vmem_limit_bytes=VMEM_BYTES

time: 17.5 us -> 17.9 us (1.023)
  Pallas kernels: 16.7 us -> 17.1 us
    pallas_call x1, Pallas kernels: 16.7 us -> 17.1 us  [local(): pl.pallas_call(functools.partial(kernel, n), out_shape=jax.ShapeDtypeStru...]
where the time goes in v7:
time: 17.9 us; the launch traced here: 17.7 us
  Pallas kernels  17.1 us (96%)
  local copies, waits for them, and re-layouts  0.66 us (4%)
    pallas_call x1, Pallas kernels, local(): pl.pallas_call(functools.partial(kernel, n), out_shape=jax.ShapeDtypeStru...  17.1 us
    unnamed x1, local copies, waits for them, and re-layouts  0.66 us

profile of v7, /device:TPU:1, one launch (start us, length us, event | category | flops | bytes accessed | tf_op | source)
XLA Modules:
  0.0 17.7 jit_solution(8993256006372661151)
XLA Ops:
  0.0 17.1 %shard_map.64 = bf16[12,4096]{1,0:T(8,128)(2,1)S(1)} custom-call(s32[1,5]{1,0:T(1,128)} %mu_hbm.1, s32[1,5]{1,0:T(1,128)} %bitcast.7, s32[1,5]{1,0:T(1,128)} %pos_hbm.1, bf16[24,2,128]{2,1,0:T(2,128)(2,1)} %bitcast.6, bf16[5,64,4096]{2,1,0:T(8,128)(2,1)} %tc_hbm.1, bf16[48,64,256]{2,1,0:T(8,128)(2,1)} %fit_hbm.1), custom_call_target="tpu_custom_call" | custom-call | tf_op jit(solution)/shard_map/pallas_call | solution.py:275
  17.1 0.7 %copy.8 = bf16[1,12,1,4096]{3,1,2,0:T(8,128)(2,1)} copy(bf16[1,12,1,4096]{3,1,2,0:T(8,128)(2,1)S(1)} %bitcast.5) | data formatting | bytes 196608

commit v8 on v4

--- a/solution.py
+++ b/solution.py
@@ -43,6 +43,18 @@
     rows = width // LANES
     groups = coeff_ref.shape[1]
 
+    barrier = pltpu.get_barrier_semaphore()
+
+    def greet(d, carry):
+        pl.semaphore_signal(
+            barrier, inc=1, device_id={"mu": lax.rem(me + d + 1, n)}, device_id_type=MESH
+        )
+        return carry
+
+    loop(n - 1, greet, 0)
+    for peer in (sibling, across, diagonal):
+        pl.semaphore_signal(barrier, inc=1, device_id={"pa": peer}, device_id_type=MESH)
+
     def tc_copy(c):
         columns = pl.ds(c * width, width)
         return pltpu.make_async_copy(
@@ -64,18 +76,6 @@
         fit_hbm.at[pl.ds(site * NU_SITE, NU_SITE)], fit, fit_sem
     )
     fit_copy.start()
-
-    barrier = pltpu.get_barrier_semaphore()
-
-    def greet(d, carry):
-        pl.semaphore_signal(
-            barrier, inc=1, device_id={"mu": lax.rem(me + d + 1, n)}, device_id_type=MESH
-        )
-        return carry
-
-    loop(n - 1, greet, 0)
-    for peer in (sibling, across, diagonal):
-        pl.semaphore_signal(barrier, inc=1, device_id={"pa": peer}, device_id_type=MESH)
 
     for copy in small:
         copy.wait()
@@ -169,11 +169,10 @@
                 return carry
             lax.fori_loop(1, n, body, 0)
 
+    pl.semaphore_wait(barrier, n - 1 + 3)
+    each_peer(lambda d: key_copy(d).start())
     for c in range(CHUNKS):
         make_payload(c)
-        if c == 0:
-            pl.semaphore_wait(barrier, n - 1 + 3)
-            each_peer(lambda d: key_copy(d).start())
         each_peer(lambda d, c=c: pay_copy(c, d).start())
 
     fit_copy.wait()

time: 17.3 us -> 17.3 us (level)
  no operation moved by 1% of the time
where the time goes in v8:
time: 17.3 us; the launch traced here: 17.1 us
  Pallas kernels  16.5 us (95%)
  local copies, waits for them, and re-layouts  0.66 us (4%)
    pallas_call x1, Pallas kernels, local(): pl.pallas_call(functools.partial(kernel, n), out_shape=jax.ShapeDtypeStru...  16.5 us
    unnamed x1, local copies, waits for them, and re-layouts  0.66 us

profile of v8, /device:TPU:1, one launch (start us, length us, event | category | flops | bytes accessed | tf_op | source)
XLA Modules:
  0.0 17.1 jit_solution(3948061120419124558)
XLA Ops:
  0.0 16.5 %shard_map.64 = bf16[12,4096]{1,0:T(8,128)(2,1)S(1)} custom-call(s32[1,5]{1,0:T(1,128)} %mu_hbm.1, s32[1,5]{1,0:T(1,128)} %bitcast.7, s32[1,5]{1,0:T(1,128)} %pos_hbm.1, bf16[24,2,128]{2,1,0:T(2,128)(2,1)} %bitcast.6, bf16[5,64,4096]{2,1,0:T(8,128)(2,1)} %tc_hbm.1, bf16[48,64,256]{2,1,0:T(8,128)(2,1)} %fit_hbm.1), custom_call_target="tpu_custom_call" | custom-call | tf_op jit(solution)/shard_map/pallas_call | solution.py:278
  16.5 0.7 %copy.8 = bf16[1,12,1,4096]{3,1,2,0:T(8,128)(2,1)} copy(bf16[1,12,1,4096]{3,1,2,0:T(8,128)(2,1)S(1)} %bitcast.5) | data formatting | bytes 196608

commit v9 on v4

--- a/solution.py
+++ b/solution.py
@@ -241,12 +241,14 @@
 
     for c in range(CHUNKS):
         sib_copy(c).wait_recv()
+    x_copy(0).wait_recv()
+    fwd_copy(0).start()
     first = 2 * lax.div(shard, 2)
     for k in range(NU_SITE):
         pair = jnp.concatenate([lines(k, first), lines(k, first + 1)], axis=1)
         held = weights[k, pl.ds(first, 2)].reshape(4 * block, LANES)
         total[k] = jnp.dot(pair, held, preferred_element_type=F32)
-    for c in range(CHUNKS):
+    for c in range(1, CHUNKS):
         x_copy(c).wait_recv()
         fwd_copy(c).start()
     for k in range(NU_SITE):

time: 17.3 us -> 17.3 us (level)
  no operation moved by 1% of the time
where the time goes in v9:
time: 17.3 us; the launch traced here: 17.2 us
  Pallas kernels  16.5 us (95%)
  local copies, waits for them, and re-layouts  0.66 us (4%)
    pallas_call x1, Pallas kernels, local(): pl.pallas_call(functools.partial(kernel, n), out_shape=jax.ShapeDtypeStru...  16.5 us
    unnamed x1, local copies, waits for them, and re-layouts  0.66 us

profile of v9, /device:TPU:1, one launch (start us, length us, event | category | flops | bytes accessed | tf_op | source)
XLA Modules:
  0.0 17.2 jit_solution(15786187895556184302)
XLA Ops:
  0.0 16.5 %shard_map.64 = bf16[12,4096]{1,0:T(8,128)(2,1)S(1)} custom-call(s32[1,5]{1,0:T(1,128)} %mu_hbm.1, s32[1,5]{1,0:T(1,128)} %bitcast.7, s32[1,5]{1,0:T(1,128)} %pos_hbm.1, bf16[24,2,128]{2,1,0:T(2,128)(2,1)} %bitcast.6, bf16[5,64,4096]{2,1,0:T(8,128)(2,1)} %tc_hbm.1, bf16[48,64,256]{2,1,0:T(8,128)(2,1)} %fit_hbm.1), custom_call_target="tpu_custom_call" | custom-call | tf_op jit(solution)/shard_map/pallas_call | solution.py:281
  16.5 0.7 %copy.8 = bf16[1,12,1,4096]{3,1,2,0:T(8,128)(2,1)} copy(bf16[1,12,1,4096]{3,1,2,0:T(8,128)(2,1)S(1)} %bitcast.5) | data formatting | bytes 196608
